TPU v7x, 256 devices: a whole 4x4x8 slice. The times are simulated.
256 devices in a mesh: ctx: 64 (over x, z, core), tp: 4 (over y).
Axes of the slice: x: 4, y: 4, z: 8, core: 2. Of those that a mesh axis runs over, the one named last changes fastest.
Arguments:
- queries: bfloat16 [64, 2, 256, 2048], P('ctx', None, None, 'tp'), may hold values from -6 to 6
- keys: bfloat16 [64, 2, 256, 512], P('ctx', None, None, 'tp'), may hold values from -6 to 6
- values: bfloat16 [64, 2, 256, 512], P('ctx', None, None, 'tp'), may hold values from -24 to 24
- column_block_table: int32 [4, 64], P('tp'), may hold values from 0 to 255, as said below
- slash_offsets: int32 [16, 64], P('tp'), may hold values from 1 to 256, as said below
- out_weight: bfloat16 [2048, 4096], P('tp'), may hold values from -0.125 to 0.125
Outputs:
- mixed: bfloat16 [64, 2, 256, 4096], P('ctx', None, None, 'tp')
Inputs may be any that keep to these rules, and one draw needn't show every extreme that they name: `column_block_table`: each row holds 64 distinct block numbers below 256, block b holding positions b * 128 to b * 128 + 127 and lying on the ctx device that holds its stretch. For each row, a quarter of the ctx devices hold exactly 2 of its blocks, half hold exactly one, the rest none. `slash_offsets`: each row holds 64 distinct offsets, and 1 and 256 are in every row.
All inputs are finite; a program needn't handle non-finite values.
Results may differ from a plain program's by a relative error of at most 0.00185.
The roundings to bfloat16 on the way count: a program that leaves them out, or rounds other values in their place, can miss the bound.
Values may be sent and summed in bfloat16 or wider, within the bound.
No kernel may reach another device: no remote copies, remote signals or barrier semaphores. Data moves between devices by JAX's collectives and lax.ppermute only.
A program may use at most 128 MiB of HBM per device.

v0:
```python
import jax
import jax.numpy as jnp
from jax import lax
from jax.sharding import PartitionSpec as P

HEAD_SIZE = 128
KEY_BLOCK_TOKENS = 128
CAP = 2


def passed_along(block, axis, distance):
    devices = range(lax.axis_size(axis))
    route = [(i - distance, i) for i in devices if i - distance in devices]
    return lax.ppermute(block, axis, route)


def owner_place(blocks, stretch_blocks, ctx_count):
    stretch_index = blocks // stretch_blocks
    first_half = stretch_index < ctx_count
    owner_device = jnp.where(first_half, stretch_index, 2 * ctx_count - 1 - stretch_index)
    local_index = jnp.where(first_half, 0, stretch_blocks) + blocks % stretch_blocks
    return (owner_device, local_index)


def slash_masks(offsets, stretch_len):
    span = 3 * stretch_len - 1
    relative = 2 * stretch_len - 1 - jnp.arange(span, dtype=jnp.int32)
    table = (
        jnp.any(relative[None, None, :] == offsets[:, :, None], axis=1) | (relative == 0)[None, :]
    )
    padded = jnp.concatenate([table, jnp.zeros((offsets.shape[0], 1), jnp.bool_)], axis=1)
    tiled = jnp.tile(padded, (1, stretch_len))[:, : stretch_len * span]
    rolled = tiled.reshape(offsets.shape[0], stretch_len, span)
    return rolled[:, :, stretch_len - 1 : 3 * stretch_len - 1]


def per_device(queries, keys, values, column_block_table, slash_offsets, out_weight):
    ctx_count = lax.axis_size("ctx")
    ctx_index = lax.axis_index("ctx")
    stretch_len = keys.shape[2]
    groups = keys.shape[3] // HEAD_SIZE
    heads = queries.shape[3] // HEAD_SIZE
    heads_per_group = heads // groups
    stretch_blocks = stretch_len // KEY_BLOCK_TOKENS
    listed = column_block_table.shape[1]
    scale = HEAD_SIZE ** (-0.5)
    kv_halves = jnp.stack([keys[0], values[0]], axis=1)
    local_blocks = kv_halves.reshape(2, 2, stretch_blocks, KEY_BLOCK_TOKENS, groups, HEAD_SIZE)
    local_blocks = local_blocks.transpose(4, 1, 0, 2, 3, 5).reshape(
        groups, 2, 2 * stretch_blocks, KEY_BLOCK_TOKENS, HEAD_SIZE
    )
    owner_device, local_index = owner_place(column_block_table, stretch_blocks, ctx_count)
    owned_here = owner_device == ctx_index
    same_owner = owner_device[:, :, None] == owner_device[:, None, :]
    position = jnp.arange(listed, dtype=jnp.int32)
    earlier = position[None, :] < position[:, None]
    owner_rank = jnp.sum(same_owner & earlier[None], axis=2)
    chosen_local = []
    chosen_valid = []
    for slot_rank in range(CAP):
        slot_hit = owned_here & (owner_rank == slot_rank)
        chosen_local.append(jnp.sum(jnp.where(slot_hit, local_index, 0), axis=1))
        chosen_valid.append(jnp.any(slot_hit, axis=1))
    chosen_local = jnp.stack(chosen_local, axis=1)
    chosen_valid = jnp.stack(chosen_valid, axis=1)
    outgoing = jnp.take_along_axis(local_blocks, chosen_local[:, None, :, None, None], axis=2)
    outgoing = jnp.where(
        chosen_valid[:, None, :, None, None], outgoing, jnp.zeros((), local_blocks.dtype)
    )
    arrived = lax.all_gather(outgoing, "ctx", axis=2, tiled=True)
    slot_index = owner_device * CAP + owner_rank
    column_kv = jnp.take_along_axis(arrived, slot_index[:, None, :, None, None], axis=2)
    before = passed_along(kv_halves[0], "ctx", 1)
    after = passed_along(kv_halves[1], "ctx", -1)
    after = jnp.where(ctx_index == ctx_count - 1, kv_halves[0], after)
    band_kv = jnp.concatenate([jnp.stack([before, after]), kv_halves], axis=2)
    stretch_ids = jnp.stack([ctx_index, 2 * ctx_count - 1 - ctx_index])
    query_pos = (
        stretch_ids[:, None] * stretch_len + jnp.arange(stretch_len, dtype=jnp.int32)[None, :]
    )
    flat_pos = query_pos.reshape(2 * stretch_len)
    band_pos = (stretch_ids[:, None] - 1) * stretch_len + jnp.arange(
        2 * stretch_len, dtype=jnp.int32
    )[None, :]
    band_listed = jnp.any(
        (band_pos // KEY_BLOCK_TOKENS)[None, :, :, None] == column_block_table[:, None, None, :],
        axis=3,
    )
    band_open = (band_pos >= 0)[None] & jnp.logical_not(band_listed)
    column_position = (
        column_block_table[:, :, None] * KEY_BLOCK_TOKENS
        + jnp.arange(KEY_BLOCK_TOKENS, dtype=jnp.int32)[None, None, :]
    ).reshape(groups, listed * KEY_BLOCK_TOKENS)
    slash_ok = slash_masks(slash_offsets, stretch_len)
    head_query = queries[0].reshape(2, stretch_len, heads, HEAD_SIZE).transpose(2, 0, 1, 3)
    column_keys = column_kv[:, 0].reshape(groups, listed * KEY_BLOCK_TOKENS, HEAD_SIZE)
    column_vals = column_kv[:, 1].reshape(groups, listed * KEY_BLOCK_TOKENS, HEAD_SIZE)
    band_keys = band_kv[:, 0].reshape(2, 2 * stretch_len, groups, HEAD_SIZE)
    band_vals = band_kv[:, 1].reshape(2, 2 * stretch_len, groups, HEAD_SIZE)

    def attend_head(inputs):
        one_query, one_slash, head_number = inputs
        group_number = head_number // heads_per_group
        keys_col = lax.dynamic_index_in_dim(column_keys, group_number, 0, keepdims=False)
        vals_col = lax.dynamic_index_in_dim(column_vals, group_number, 0, keepdims=False)
        keys_band = lax.dynamic_index_in_dim(band_keys, group_number, 2, keepdims=False)
        vals_band = lax.dynamic_index_in_dim(band_vals, group_number, 2, keepdims=False)
        open_band = lax.dynamic_index_in_dim(band_open, group_number, 0, keepdims=False)
        pos_col = lax.dynamic_index_in_dim(column_position, group_number, 0, keepdims=False)
        flat_query = one_query.reshape(2 * stretch_len, HEAD_SIZE)
        col_scores = (
            jnp.einsum("id,jd->ij", flat_query, keys_col, preferred_element_type=jnp.float32)
            * scale
        )
        col_mask = pos_col[None, :] <= flat_pos[:, None]
        band_scores = (
            jnp.einsum("hid,hjd->hij", one_query, keys_band, preferred_element_type=jnp.float32)
            * scale
        )
        band_mask = one_slash[None] & open_band[:, None, :]
        col_max = jnp.max(jnp.where(col_mask, col_scores, -jnp.inf), axis=1).reshape(2, stretch_len)
        band_max = jnp.max(jnp.where(band_mask, band_scores, -jnp.inf), axis=2)
        row_max = jnp.maximum(col_max, band_max)
        col_exp = jnp.where(
            col_mask, jnp.exp(col_scores - row_max.reshape(2 * stretch_len)[:, None]), 0.0
        )
        band_exp = jnp.where(band_mask, jnp.exp(band_scores - row_max[:, :, None]), 0.0)
        row_total = jnp.sum(col_exp, axis=1).reshape(2, stretch_len) + jnp.sum(band_exp, axis=2)
        weighted = jnp.dot(
            col_exp.astype(jnp.bfloat16), vals_col, preferred_element_type=jnp.float32
        ).reshape(2, stretch_len, HEAD_SIZE)
        weighted = weighted + jnp.einsum(
            "hij,hjd->hid",
            band_exp.astype(jnp.bfloat16),
            vals_band,
            preferred_element_type=jnp.float32,
        )
        return (weighted / row_total[:, :, None]).astype(jnp.bfloat16)

    head_out = lax.map(attend_head, (head_query, slash_ok, jnp.arange(heads, dtype=jnp.int32)))
    attended = head_out.transpose(1, 2, 0, 3).reshape(2, stretch_len, heads * HEAD_SIZE)
    partial_out = jnp.einsum(
        "hic,cd->hid", attended, out_weight, preferred_element_type=jnp.float32
    )
    mixed = lax.psum_scatter(partial_out, "tp", scatter_dimension=2, tiled=True).astype(
        jnp.bfloat16
    )
    return mixed[None]


def solution(mesh):
    in_specs = (
        P("ctx", None, None, "tp"),
        P("ctx", None, None, "tp"),
        P("ctx", None, None, "tp"),
        P("tp", None),
        P("tp", None),
        P("tp", None),
    )
    out_specs = P("ctx", None, None, "tp")
    return jax.shard_map(
        per_device, mesh=mesh, in_specs=in_specs, out_specs=out_specs, check_vma=False
    )
```

profile of v0, /device:TPU:1, one launch (start us, length us, event | category | flops | bytes accessed | tf_op | source)
XLA Modules:
  0.0 334.6 jit_solution(4886587028446778955)
XLA Ops:
  6.5 0.7 fusion.34
  7.3 0.2 convert_reduce_fusion
  7.4 0.7 fusion.40
  8.2 0.7 select_reduce_fusion.1
  8.8 1.3 fusion.35
  10.1 1.3 compare_and_fusion
  11.4 1.0 pad_maximum_fusion
  12.4 0.6 gather_fusion
  13.0 1.4 add_bitcast_fusion.1
  14.4 0.7 fusion.32
  15.2 0.9 fusion.30
  16.1 5.1 %collective-permute-start.1 = (bf16[2,256,128]{2,1,0:T(8,128)(2,1)S(1)}, bf16[2,256,128]{2,1,0:T(8,128)(2,1)S(1)}, u32[]{:S(2)}, u32[]{:S(2)}) collective-permute-start(bf16[2,256,128]{2,1,0:T(8,128)(2,1)S(1)} %fusion.30), channel_id=1, source_target_pairs={{4,0},{8,4},{12,8},{16,12},{20,16},{24,20},{28,24},{32,28},{36,32}... | collective-permute-start | bytes 393224 | tf_op jit(solution)/shard_map/ppermute | solution.py:14
  21.3 0.9 compare_reduce_fusion
  22.3 0.8 compare_reduce_fusion.1
  23.1 0.6 fusion.36
  23.8 0.2 broadcast_bitcast_fusion
  24.0 0.5 compare_and_fusion.3
  24.5 0.9 select_bitcast_fusion
  25.4 1.9 collective-permute-start
  27.3 0.7 broadcast_multiply_fusion.1
  28.0 1.0 copy.51
  28.9 0.9 slice.38
  29.8 0.7 reshape.531
  30.5 3.7 %reshape.503 = pred[4,256,767]{2,1,0:T(8,128)(4,1)S(1)} reshape(pred[785408]{0:T(1024)(128)(4,1)S(1)} %reshape.531) | data formatting | bytes 1570816 | tf_op jit(solution)/shard_map/reshape | solution.py:33
  34.2 0.7 slice.39
  34.9 1.2 copy.34
  36.1 0.7 pad_clamp_fusion
  36.8 0.9 maximum_maximum_fusion
  37.8 64.7 %all-gather.2.cloned.1.call-done = bf16[1,2,128,128,128]{4,3,1,0,2:T(8,128)(2,1)} async-done(((bf16[1,2,2,128,128]{4,3,1,0,2:T(8,128)(2,1)}), bf16[1,2,128,128,128]{4,3,1,0,2:T(8,128)(2,1)}) %all-gather.2.cloned.1.call-update) | async-done | bytes 8388624 | tf_op jit(solution)/shard_map/all_gather | solution.py:70
  102.5 10.3 %copy.55 = bf16[1,2,128,128,128]{4,3,2,1,0:T(8,128)(2,1)} copy(bf16[1,2,128,128,128]{4,3,1,0,2:T(8,128)(2,1)} %all-gather.2.cloned.1.call-done) | data formatting | bytes 16777216 | tf_op jit(solution)/shard_map/all_gather | solution.py:70
  112.9 6.4 %gather_fusion.1 = bf16[64,2,128,128]{3,2,1,0:T(8,128)(2,1)} fusion(bf16[2,128,128,128]{3,2,1,0:T(8,128)(2,1)} %bitcast.175, s32[1024]{0:T(1024)S(1)} %pad_clamp_fusion), kind=kCustom, calls=%fused_computation.1 | custom fusion | bytes 8388864 | tf_op jit(solution)/shard_map/jit(take_along_axis)/gather | solution.py:72
  119.3 2.6 bitcast_select_fusion
  121.9 2.5 fusion.41
  124.4 112.7 %while.12 = (s32[]{:T(128)}, bf16[4,2,256,128]{2,3,0,1:T(8,128)(2,1)S(1)}, bf16[4,2,256,128]{2,3,0,1:T(8,128)(2,1)S(1)}, bf16[1,8192,128]{2,1,0:T(8,128)(2,1)}, ...) while((s32[]{:T(128)}, ...), condition=%wide.region_12.13_spmd.clone, body=%wide.region_7.12_spmd.clone.sunk | while | flops 2326994944 | bytes 61042056 | solution.py:140
  124.4 0.5 fusion.63
  125.3 8.7 %fusion.62 = (f32[512]{0:T(512)S(1)}, f32[512,8192]{1,0:T(8,128)}) fusion(s32[8192]{0:T(1024)S(1)} %bitcast.176, s32[512]{0:T(512)S(1)} %bitcast.194, bf16[512,128]{1,0:T(8,128)(2,1)S(1)} %bitcast.178, bf16[1,8192,128]{2,1,0:T(8,128)(2,1)} %get-tuple-element.312), kind=kOutput, calls=%fused_computation.6.clone.1 | convolution fusion | flops 1090518528 | bytes 19042304 | tf_op jit(solution)/shard_map/while/body/eval_jaxpr/id,jd->ij/dot_general | solution.py:112
  133.9 0.4 fusion.66
  134.4 11.2 %fusion.64 = (f32[512]{0:T(512)S(1)}, bf16[512,8192]{1,0:T(8,128)(2,1)}) fusion(f32[512,8192]{1,0:T(8,128)} %get-tuple-element.279, f32[512]{0:T(512)S(1)} %max.19, s32[8192]{0:T(1024)S(1)} %bitcast.177, s32[512]{0:T(512)S(1)} %bitcast.195), kind=kLoop, calls=%fused_computation.7.clone.1 | loop fusion | flops 25165312 | bytes 25204736 | tf_op jit(solution)/shard_map/while/body/eval_jaxpr/reduce_sum | solution.py:128
  145.6 6.3 %fusion.65 = f32[2,256,128]{2,1,0:T(8,128)S(1)} fusion(bf16[2,256,8192]{2,1,0:T(8,128)(2,1)} %bitcast.174, bf16[1,8192,128]{2,1,0:T(8,128)(2,1)} %get-tuple-element.316), kind=kOutput, calls=%fused_computation.9.clone.1 | convolution fusion | flops 1073741824 | bytes 10747904 | tf_op jit(solution)/shard_map/while/body/eval_jaxpr/dot_general | solution.py:129
  151.9 0.4 fusion.67
  152.6 0.5 fusion.63
  153.2 0.1 bitcast_add_fusion.3
  153.4 8.7 %fusion.62 = (f32[512]{0:T(512)S(1)}, f32[512,8192]{1,0:T(8,128)}) fusion(s32[8192]{0:T(1024)S(1)} %bitcast.176, s32[512]{0:T(512)S(1)} %bitcast.194, bf16[512,128]{1,0:T(8,128)(2,1)S(1)} %bitcast.178, bf16[1,8192,128]{2,1,0:T(8,128)(2,1)} %get-tuple-element.312), kind=kOutput, calls=%fused_computation.6.clone.1 | convolution fusion | flops 1090518528 | bytes 19042304 | tf_op jit(solution)/shard_map/while/body/eval_jaxpr/id,jd->ij/dot_general | solution.py:112
  162.1 0.4 fusion.66
  162.5 11.2 %fusion.64 = (f32[512]{0:T(512)S(1)}, bf16[512,8192]{1,0:T(8,128)(2,1)}) fusion(f32[512,8192]{1,0:T(8,128)} %get-tuple-element.279, f32[512]{0:T(512)S(1)} %max.19, s32[8192]{0:T(1024)S(1)} %bitcast.177, s32[512]{0:T(512)S(1)} %bitcast.195), kind=kLoop, calls=%fused_computation.7.clone.1 | loop fusion | flops 25165312 | bytes 25204736 | tf_op jit(solution)/shard_map/while/body/eval_jaxpr/reduce_sum | solution.py:128
  173.8 6.3 %fusion.65 = f32[2,256,128]{2,1,0:T(8,128)S(1)} fusion(bf16[2,256,8192]{2,1,0:T(8,128)(2,1)} %bitcast.174, bf16[1,8192,128]{2,1,0:T(8,128)(2,1)} %get-tuple-element.316), kind=kOutput, calls=%fused_computation.9.clone.1 | convolution fusion | flops 1073741824 | bytes 10747904 | tf_op jit(solution)/shard_map/while/body/eval_jaxpr/dot_general | solution.py:129
  180.1 0.4 fusion.67
  180.8 0.5 fusion.63
  181.4 0.1 bitcast_add_fusion.3
  181.6 8.7 %fusion.62 = (f32[512]{0:T(512)S(1)}, f32[512,8192]{1,0:T(8,128)}) fusion(s32[8192]{0:T(1024)S(1)} %bitcast.176, s32[512]{0:T(512)S(1)} %bitcast.194, bf16[512,128]{1,0:T(8,128)(2,1)S(1)} %bitcast.178, bf16[1,8192,128]{2,1,0:T(8,128)(2,1)} %get-tuple-element.312), kind=kOutput, calls=%fused_computation.6.clone.1 | convolution fusion | flops 1090518528 | bytes 19042304 | tf_op jit(solution)/shard_map/while/body/eval_jaxpr/id,jd->ij/dot_general | solution.py:112
  190.3 0.4 fusion.66
  190.7 11.2 %fusion.64 = (f32[512]{0:T(512)S(1)}, bf16[512,8192]{1,0:T(8,128)(2,1)}) fusion(f32[512,8192]{1,0:T(8,128)} %get-tuple-element.279, f32[512]{0:T(512)S(1)} %max.19, s32[8192]{0:T(1024)S(1)} %bitcast.177, s32[512]{0:T(512)S(1)} %bitcast.195), kind=kLoop, calls=%fused_computation.7.clone.1 | loop fusion | flops 25165312 | bytes 25204736 | tf_op jit(solution)/shard_map/while/body/eval_jaxpr/reduce_sum | solution.py:128
  202.0 6.3 %fusion.65 = f32[2,256,128]{2,1,0:T(8,128)S(1)} fusion(bf16[2,256,8192]{2,1,0:T(8,128)(2,1)} %bitcast.174, bf16[1,8192,128]{2,1,0:T(8,128)(2,1)} %get-tuple-element.316), kind=kOutput, calls=%fused_computation.9.clone.1 | convolution fusion | flops 1073741824 | bytes 10747904 | tf_op jit(solution)/shard_map/while/body/eval_jaxpr/dot_general | solution.py:129
  208.3 0.4 fusion.67
  208.9 0.5 fusion.63
  209.6 0.1 bitcast_add_fusion.3
  209.8 8.7 %fusion.62 = (f32[512]{0:T(512)S(1)}, f32[512,8192]{1,0:T(8,128)}) fusion(s32[8192]{0:T(1024)S(1)} %bitcast.176, s32[512]{0:T(512)S(1)} %bitcast.194, bf16[512,128]{1,0:T(8,128)(2,1)S(1)} %bitcast.178, bf16[1,8192,128]{2,1,0:T(8,128)(2,1)} %get-tuple-element.312), kind=kOutput, calls=%fused_computation.6.clone.1 | convolution fusion | flops 1090518528 | bytes 19042304 | tf_op jit(solution)/shard_map/while/body/eval_jaxpr/id,jd->ij/dot_general | solution.py:112
  218.5 0.4 fusion.66
  218.9 11.2 %fusion.64 = (f32[512]{0:T(512)S(1)}, bf16[512,8192]{1,0:T(8,128)(2,1)}) fusion(f32[512,8192]{1,0:T(8,128)} %get-tuple-element.279, f32[512]{0:T(512)S(1)} %max.19, s32[8192]{0:T(1024)S(1)} %bitcast.177, s32[512]{0:T(512)S(1)} %bitcast.195), kind=kLoop, calls=%fused_computation.7.clone.1 | loop fusion | flops 25165312 | bytes 25204736 | tf_op jit(solution)/shard_map/while/body/eval_jaxpr/reduce_sum | solution.py:128
  230.2 6.3 %fusion.65 = f32[2,256,128]{2,1,0:T(8,128)S(1)} fusion(bf16[2,256,8192]{2,1,0:T(8,128)(2,1)} %bitcast.174, bf16[1,8192,128]{2,1,0:T(8,128)(2,1)} %get-tuple-element.316), kind=kOutput, calls=%fused_computation.9.clone.1 | convolution fusion | flops 1073741824 | bytes 10747904 | tf_op jit(solution)/shard_map/while/body/eval_jaxpr/dot_general | solution.py:129
  236.5 0.4 fusion.67
  237.1 7.8 %fusion.26 = f32[2,256,4096]{2,1,0:T(8,128)} fusion(bf16[2,256,512]{1,2,0:T(8,128)(2,1)S(1)} %bitcast.193, bf16[512,4096]{1,0:T(8,128)(2,1)} %param.13), kind=kOutput, calls=%fused_computation.38 | convolution fusion | flops 2147483648 | bytes 13107200 | tf_op jit(solution)/shard_map/hic,cd->hid/dot_general | solution.py:142
  244.9 80.2 %reduce-scatter.2.cloned.1.call-done = f32[2,256,1024]{2,1,0:T(8,128)} async-done(((f32[2,256,4096]{2,1,0:T(8,128)}), f32[2,256,1024]{2,1,0:T(8,128)}) %reduce-scatter.2.cloned.1.call-update) | async-done | bytes 2097168 | tf_op jit(solution)/shard_map/reduce_scatter | solution.py:145
  325.0 2.7 convert_bitcast_fusion
  (80 shorter events, 2.2 us)
Async XLA Ops:
  6.5 30.3 %copy-start.1 = (bf16[1,2,256,128]{3,2,1,0:T(8,128)(2,1)S(1)}, bf16[1,2,256,128]{3,2,1,0:T(8,128)(2,1)}, u32[]{:S(2)}) copy-start(bf16[1,2,256,128]{3,2,1,0:T(8,128)(2,1)} %param.9) | copy-start | bytes 393220
  6.5 30.3 %copy-start = (bf16[1,2,256,128]{3,2,1,0:T(8,128)(2,1)S(1)}, bf16[1,2,256,128]{3,2,1,0:T(8,128)(2,1)}, u32[]{:S(2)}) copy-start(bf16[1,2,256,128]{3,2,1,0:T(8,128)(2,1)} %param.10) | copy-start | bytes 393220
  6.5 96.0 %all-gather.2.cloned.1.call-start = ((), (), s32[]{:S(2)}) async-start(), calls=%async_computation.1 | async-start | bytes 8519680 | tf_op jit(solution)/shard_map/all_gather | solution.py:70
  15.1 309.9 %reduce-scatter.2.cloned.1.call-start = ((), (), s32[]{:S(2)}) async-start(), calls=%async_computation.2 | async-start | bytes 10485760 | tf_op jit(solution)/shard_map/reduce_scatter | solution.py:145
  16.1 8.4 %collective-permute-start.1 = (bf16[2,256,128]{2,1,0:T(8,128)(2,1)S(1)}, bf16[2,256,128]{2,1,0:T(8,128)(2,1)S(1)}, u32[]{:S(2)}, u32[]{:S(2)}) collective-permute-start(bf16[2,256,128]{2,1,0:T(8,128)(2,1)S(1)} %fusion.30), channel_id=1, source_target_pairs={{4,0},{8,4},{12,8},{16,12},{20,16},{24,20},{28,24},{32,28},{36,32}... | collective-permute-start | bytes 393224 | tf_op jit(solution)/shard_map/ppermute | solution.py:14
  25.4 11.4 %collective-permute-start = (bf16[2,256,128]{2,1,0:T(8,128)(2,1)S(1)}, bf16[2,256,128]{2,1,0:T(8,128)(2,1)}, u32[]{:S(2)}, u32[]{:S(2)}) collective-permute-start(bf16[2,256,128]{2,1,0:T(8,128)(2,1)S(1)} %get-tuple-element.185), channel_id=1, source_target_pairs={{0,4},{4,8},{8,12},{12,16},{16,20},{20,24},{24,28},{28,32},{32,36}... | collective-permute-start | bytes 393224 | tf_op jit(solution)/shard_map/ppermute | solution.py:14
  112.9 6.4 %copy-start.2 = (pred[64]{0:T(512)(128)(4,1)S(1)}, pred[64]{0:T(512)(128)(4,1)}, u32[]{:S(2)}) copy-start(pred[64]{0:T(512)(128)(4,1)} %compare_and_fusion.3) | copy-start | bytes 196
Sparse Core Ops, SparseCore 0:
  15.3 87.2 all-gather.1
  245.0 80.0 reduce-scatter.1
where the time goes:
time: 335 us
  waiting for transfers between devices  145 us (43%)
  matrix products  71.3 us (21%)
  other arithmetic  67.9 us (20%)
  local copies, waits for them, and re-layouts  29.5 us (9%)
  between operations  13.6 us (4%)
  starting transfers between devices  7.11 us (2%)
    reduce_scatter x1, waiting for transfers between devices, per_device(): lax.psum_scatter(partial_out, 'tp', scatter_dimension=2, tiled=True)  80.2 us
    all_gather x1, waiting for transfers between devices, per_device(): arrived = lax.all_gather(outgoing, 'ctx', axis=2, tiled=True)  64.7 us
    reduce_sum x4, other arithmetic, attend_head(): jnp.sum(col_exp, axis=1).reshape(2, stretch_len) + jnp.sum(band_exp, axis=2)  45 us
    dot_general x4, matrix products, attend_head(): jnp.einsum('id,jd->ij', flat_query, keys_col, preferred_element_type=jnp....  34.7 us
    dot_general x4, matrix products, attend_head(): jnp.dot(col_exp.astype(jnp.bfloat16), vals_col, preferred_element_type=jn...  25.2 us
    all_gather x1, local copies, waits for them, and re-layouts, per_device(): arrived = lax.all_gather(outgoing, 'ctx', axis=2, tiled=True)  10.3 us
    dot_general x1, matrix products, per_device(): jnp.einsum('hic,cd->hid', attended, out_weight, preferred_element_type=jn...  7.79 us
    ppermute x2, starting transfers between devices, passed_along(): return lax.ppermute(block, axis, route)  7.07 us
  transfers between devices with their start and end apart: 4, of which 2 were waited for; matrix products, arithmetic and copies ran while one was open for 5% of the time, Pallas kernels for 0%

commit v1 on v0

--- a/solution.py
+++ b/solution.py
@@ -67,7 +67,9 @@
     outgoing = jnp.where(
         chosen_valid[:, None, :, None, None], outgoing, jnp.zeros((), local_blocks.dtype)
     )
-    arrived = lax.all_gather(outgoing, "ctx", axis=2, tiled=True)
+    arrived = jnp.concatenate(
+        lax.all_to_all(jnp.stack([outgoing] * lax.axis_size("ctx")), "ctx", 0, 0), axis=2
+    )
     slot_index = owner_device * CAP + owner_rank
     column_kv = jnp.take_along_axis(arrived, slot_index[:, None, :, None, None], axis=2)
     before = passed_along(kv_halves[0], "ctx", 1)

time: 335 us -> 464 us (1.39)
  waiting for transfers between devices: 145 us -> 262 us
  starting transfers between devices: 7.11 us -> 17.9 us
  local copies, waits for them, and re-layouts: 29.5 us -> 34.8 us
    ppermute x2, waiting for transfers between devices: 0.01 us -> 179 us  [passed_along(): return lax.ppermute(block, axis, route)]
    all_gather x1 -> x0, waiting for transfers between devices: 64.7 us -> none  [per_device(): arrived = lax.all_gather(outgoing, 'ctx', axis=2, tiled=True)]
    all_to_all x0 -> x1, starting transfers between devices: none -> 13.3 us  [per_device(): lax.all_to_all(jnp.stack([outgoing] * lax.axis_size('ctx')), 'ctx', 0, 0)]
    all_to_all x0 -> x1, local copies, waits for them, and re-layouts: none -> 10.3 us  [per_device(): lax.all_to_all(jnp.stack([outgoing] * lax.axis_size('ctx')), 'ctx', 0, 0)]
    all_gather x1 -> x0, local copies, waits for them, and re-layouts: 10.3 us -> none  [per_device(): arrived = lax.all_gather(outgoing, 'ctx', axis=2, tiled=True)]
    another operation x0 -> x1, local copies, waits for them, and re-layouts: none -> 5.34 us  [per_device(): jnp.stack([outgoing] * lax.axis_size('ctx'))]
  transfers between devices with their start and end apart: 4 -> 4, of which waited for: 2 -> 2; matrix products, arithmetic and copies ran while one was open for 5% -> 3% of each run, Pallas kernels for 0% -> 0%
where the time goes in v1:
time: 464 us
  waiting for transfers between devices  262 us (56%)
  matrix products  71.3 us (15%)
  other arithmetic  63.4 us (14%)
  local copies, waits for them, and re-layouts  34.8 us (7%)
  starting transfers between devices  17.9 us (4%)
  between operations  13.7 us (3%)
    ppermute x2, waiting for transfers between devices, passed_along(): return lax.ppermute(block, axis, route)  179 us
    reduce_scatter x1, waiting for transfers between devices, per_device(): lax.psum_scatter(partial_out, 'tp', scatter_dimension=2, tiled=True)  82.8 us
    reduce_sum x4, other arithmetic, attend_head(): jnp.sum(col_exp, axis=1).reshape(2, stretch_len) + jnp.sum(band_exp, axis=2)  45 us
    dot_general x4, matrix products, attend_head(): jnp.einsum('id,jd->ij', flat_query, keys_col, preferred_element_type=jnp....  34.7 us
    dot_general x4, matrix products, attend_head(): jnp.dot(col_exp.astype(jnp.bfloat16), vals_col, preferred_element_type=jn...  25.2 us
    all_to_all x1, starting transfers between devices, per_device(): lax.all_to_all(jnp.stack([outgoing] * lax.axis_size('ctx')), 'ctx', 0, 0)  13.3 us
    all_to_all x1, local copies, waits for them, and re-layouts, per_device(): lax.all_to_all(jnp.stack([outgoing] * lax.axis_size('ctx')), 'ctx', 0, 0)  10.3 us
  transfers between devices with their start and end apart: 4, of which 2 were waited for; matrix products, arithmetic and copies ran while one was open for 3% of the time, Pallas kernels for 0%

profile of v1, /device:TPU:1, one launch (start us, length us, event | category | flops | bytes accessed | tf_op | source)
XLA Modules:
  0.0 463.7 jit_solution(7233577716543360393)
XLA Ops:
  6.5 0.7 fusion.32
  7.2 0.2 convert_reduce_fusion
  7.4 0.7 fusion.38
  8.1 0.7 select_reduce_fusion.1
  8.8 1.3 fusion.33
  10.2 1.3 compare_and_fusion
  11.5 1.0 pad_maximum_fusion
  12.5 0.6 gather_fusion
  13.1 1.3 add_bitcast_fusion.1
  14.5 5.3 %stack.46 = bf16[64,1,2,2,128,128]{5,4,3,2,1,0:T(8,128)(2,1)} broadcast(bf16[2,2,128,128]{3,2,1,0:T(8,128)(2,1)S(1)} %copy.38), dimensions={2,3,4,5} | broadcast | bytes 8519680 | tf_op jit(solution)/shard_map/stack | solution.py:71
  19.9 13.3 %all-to-all-start = ((bf16[64,1,2,2,128,128]{5,4,3,2,1,0:T(8,128)(2,1)}), bf16[64,1,2,2,128,128]{5,4,3,2,1,0:T(8,128)(2,1)}, u32[]{:S(2)}, u32[]{:S(2)}) async-start(bf16[64,1,2,2,128,128]{5,4,3,2,1,0:T(8,128)(2,1)} %stack.46), calls=%async_computation | async-start | bytes 16777216 | tf_op jit(solution)/shard_map/all_to_all | solution.py:71
  33.3 2.4 collective-permute-start.1
  35.8 0.2 compare_reduce_fusion
  36.3 0.5 fusion.34
  36.9 0.2 broadcast_bitcast_fusion
  37.1 0.6 compare_and_fusion.3
  37.7 179.4 %collective-permute-done.1 = bf16[2,256,128]{2,1,0:T(8,128)(2,1)S(1)} collective-permute-done((bf16[2,256,128]{2,1,0:T(8,128)(2,1)S(1)}, bf16[2,256,128]{2,1,0:T(8,128)(2,1)S(1)}, u32[]{:S(2)}, u32[]{:S(2)}) %collective-permute-start.1) | collective-permute-done | bytes 131104 | tf_op jit(solution)/shard_map/ppermute | solution.py:14
  217.1 2.1 collective-permute-start
  219.2 1.0 copy.52
  220.2 0.9 slice.38
  221.1 0.7 reshape.539
  221.7 3.7 reshape.509
  225.5 0.6 slice.39
  226.1 1.2 copy.35
  227.4 0.6 pad_clamp_fusion
  228.0 0.9 maximum_maximum_fusion
  229.0 10.3 %copy.39 = bf16[64,1,2,2,128,128]{5,4,3,0,2,1:T(8,128)(2,1)} copy(bf16[64,1,2,2,128,128]{5,4,3,2,1,0:T(8,128)(2,1)} %all-to-all-done) | data formatting | bytes 16777216 | tf_op jit(solution)/shard_map/all_to_all | solution.py:71
  239.3 6.4 %gather_fusion.1 = bf16[64,2,128,128]{3,2,1,0:T(8,128)(2,1)} fusion(bf16[2,128,128,128]{3,2,1,0:T(8,128)(2,1)} %bitcast.167, s32[1024]{0:T(1024)S(1)} %pad_clamp_fusion), kind=kCustom, calls=%fused_computation.1 | custom fusion | bytes 8388864 | tf_op jit(solution)/shard_map/jit(take_along_axis)/gather | solution.py:74
  245.7 2.6 bitcast_select_fusion
  248.3 2.5 fusion.39
  250.8 112.7 %while.12 = (s32[]{:T(128)}, bf16[4,2,256,128]{2,3,0,1:T(8,128)(2,1)S(1)}, bf16[4,2,256,128]{2,3,0,1:T(8,128)(2,1)S(1)}, bf16[1,8192,128]{2,1,0:T(8,128)(2,1)}, ...) while((s32[]{:T(128)}, ...), condition=%wide.region_12.13_spmd.clone, body=%wide.region_7.12_spmd.clone.sunk | while | flops 2326994944 | bytes 61042056 | solution.py:142
  250.9 0.5 fusion.61
  251.3 0.1 copy.60
  251.5 0.1 bitcast_add_fusion.3
  251.7 8.7 %fusion.60 = (f32[512]{0:T(512)S(1)}, f32[512,8192]{1,0:T(8,128)}) fusion(s32[8192]{0:T(1024)S(1)} %bitcast.168, s32[512]{0:T(512)S(1)} %bitcast.186, bf16[512,128]{1,0:T(8,128)(2,1)S(1)} %bitcast.170, bf16[1,8192,128]{2,1,0:T(8,128)(2,1)} %get-tuple-element.312), kind=kOutput, calls=%fused_computation.6.clone.1 | convolution fusion | flops 1090518528 | bytes 19042304 | tf_op jit(solution)/shard_map/while/body/eval_jaxpr/id,jd->ij/dot_general | solution.py:114
  260.4 0.4 fusion.64
  260.8 11.2 %fusion.62 = (f32[512]{0:T(512)S(1)}, bf16[512,8192]{1,0:T(8,128)(2,1)}) fusion(f32[512,8192]{1,0:T(8,128)} %get-tuple-element.279, f32[512]{0:T(512)S(1)} %max.19, s32[8192]{0:T(1024)S(1)} %bitcast.169, s32[512]{0:T(512)S(1)} %bitcast.187), kind=kLoop, calls=%fused_computation.7.clone.1 | loop fusion | flops 25165312 | bytes 25204736 | tf_op jit(solution)/shard_map/while/body/eval_jaxpr/reduce_sum | solution.py:130
  272.1 6.3 %fusion.63 = f32[2,256,128]{2,1,0:T(8,128)S(1)} fusion(bf16[2,256,8192]{2,1,0:T(8,128)(2,1)} %bitcast.166, bf16[1,8192,128]{2,1,0:T(8,128)(2,1)} %get-tuple-element.316), kind=kOutput, calls=%fused_computation.9.clone.1 | convolution fusion | flops 1073741824 | bytes 10747904 | tf_op jit(solution)/shard_map/while/body/eval_jaxpr/dot_general | solution.py:131
  278.4 0.4 fusion.65
  279.0 0.5 fusion.61
  279.7 0.1 bitcast_add_fusion.3
  279.9 8.7 %fusion.60 = (f32[512]{0:T(512)S(1)}, f32[512,8192]{1,0:T(8,128)}) fusion(s32[8192]{0:T(1024)S(1)} %bitcast.168, s32[512]{0:T(512)S(1)} %bitcast.186, bf16[512,128]{1,0:T(8,128)(2,1)S(1)} %bitcast.170, bf16[1,8192,128]{2,1,0:T(8,128)(2,1)} %get-tuple-element.312), kind=kOutput, calls=%fused_computation.6.clone.1 | convolution fusion | flops 1090518528 | bytes 19042304 | tf_op jit(solution)/shard_map/while/body/eval_jaxpr/id,jd->ij/dot_general | solution.py:114
  288.6 0.4 fusion.64
  289.0 11.2 %fusion.62 = (f32[512]{0:T(512)S(1)}, bf16[512,8192]{1,0:T(8,128)(2,1)}) fusion(f32[512,8192]{1,0:T(8,128)} %get-tuple-element.279, f32[512]{0:T(512)S(1)} %max.19, s32[8192]{0:T(1024)S(1)} %bitcast.169, s32[512]{0:T(512)S(1)} %bitcast.187), kind=kLoop, calls=%fused_computation.7.clone.1 | loop fusion | flops 25165312 | bytes 25204736 | tf_op jit(solution)/shard_map/while/body/eval_jaxpr/reduce_sum | solution.py:130
  300.3 6.3 %fusion.63 = f32[2,256,128]{2,1,0:T(8,128)S(1)} fusion(bf16[2,256,8192]{2,1,0:T(8,128)(2,1)} %bitcast.166, bf16[1,8192,128]{2,1,0:T(8,128)(2,1)} %get-tuple-element.316), kind=kOutput, calls=%fused_computation.9.clone.1 | convolution fusion | flops 1073741824 | bytes 10747904 | tf_op jit(solution)/shard_map/while/body/eval_jaxpr/dot_general | solution.py:131
  306.6 0.4 fusion.65
  307.2 0.5 fusion.61
  307.7 0.1 copy.60
  307.8 0.1 bitcast_add_fusion.3
  308.0 8.7 %fusion.60 = (f32[512]{0:T(512)S(1)}, f32[512,8192]{1,0:T(8,128)}) fusion(s32[8192]{0:T(1024)S(1)} %bitcast.168, s32[512]{0:T(512)S(1)} %bitcast.186, bf16[512,128]{1,0:T(8,128)(2,1)S(1)} %bitcast.170, bf16[1,8192,128]{2,1,0:T(8,128)(2,1)} %get-tuple-element.312), kind=kOutput, calls=%fused_computation.6.clone.1 | convolution fusion | flops 1090518528 | bytes 19042304 | tf_op jit(solution)/shard_map/while/body/eval_jaxpr/id,jd->ij/dot_general | solution.py:114
  316.7 0.4 fusion.64
  317.2 11.2 %fusion.62 = (f32[512]{0:T(512)S(1)}, bf16[512,8192]{1,0:T(8,128)(2,1)}) fusion(f32[512,8192]{1,0:T(8,128)} %get-tuple-element.279, f32[512]{0:T(512)S(1)} %max.19, s32[8192]{0:T(1024)S(1)} %bitcast.169, s32[512]{0:T(512)S(1)} %bitcast.187), kind=kLoop, calls=%fused_computation.7.clone.1 | loop fusion | flops 25165312 | bytes 25204736 | tf_op jit(solution)/shard_map/while/body/eval_jaxpr/reduce_sum | solution.py:130
  328.4 6.3 %fusion.63 = f32[2,256,128]{2,1,0:T(8,128)S(1)} fusion(bf16[2,256,8192]{2,1,0:T(8,128)(2,1)} %bitcast.166, bf16[1,8192,128]{2,1,0:T(8,128)(2,1)} %get-tuple-element.316), kind=kOutput, calls=%fused_computation.9.clone.1 | convolution fusion | flops 1073741824 | bytes 10747904 | tf_op jit(solution)/shard_map/while/body/eval_jaxpr/dot_general | solution.py:131
  334.7 0.4 fusion.65
  335.4 0.5 fusion.61
  336.0 0.1 bitcast_add_fusion.3
  336.2 8.7 %fusion.60 = (f32[512]{0:T(512)S(1)}, f32[512,8192]{1,0:T(8,128)}) fusion(s32[8192]{0:T(1024)S(1)} %bitcast.168, s32[512]{0:T(512)S(1)} %bitcast.186, bf16[512,128]{1,0:T(8,128)(2,1)S(1)} %bitcast.170, bf16[1,8192,128]{2,1,0:T(8,128)(2,1)} %get-tuple-element.312), kind=kOutput, calls=%fused_computation.6.clone.1 | convolution fusion | flops 1090518528 | bytes 19042304 | tf_op jit(solution)/shard_map/while/body/eval_jaxpr/id,jd->ij/dot_general | solution.py:114
  344.9 0.4 fusion.64
  345.3 11.2 %fusion.62 = (f32[512]{0:T(512)S(1)}, bf16[512,8192]{1,0:T(8,128)(2,1)}) fusion(f32[512,8192]{1,0:T(8,128)} %get-tuple-element.279, f32[512]{0:T(512)S(1)} %max.19, s32[8192]{0:T(1024)S(1)} %bitcast.169, s32[512]{0:T(512)S(1)} %bitcast.187), kind=kLoop, calls=%fused_computation.7.clone.1 | loop fusion | flops 25165312 | bytes 25204736 | tf_op jit(solution)/shard_map/while/body/eval_jaxpr/reduce_sum | solution.py:130
  356.6 6.3 %fusion.63 = f32[2,256,128]{2,1,0:T(8,128)S(1)} fusion(bf16[2,256,8192]{2,1,0:T(8,128)(2,1)} %bitcast.166, bf16[1,8192,128]{2,1,0:T(8,128)(2,1)} %get-tuple-element.316), kind=kOutput, calls=%fused_computation.9.clone.1 | convolution fusion | flops 1073741824 | bytes 10747904 | tf_op jit(solution)/shard_map/while/body/eval_jaxpr/dot_general | solution.py:131
  362.9 0.4 fusion.65
  363.5 7.8 %fusion.26 = f32[2,256,4096]{2,1,0:T(8,128)} fusion(bf16[2,256,512]{1,2,0:T(8,128)(2,1)S(1)} %bitcast.185, bf16[512,4096]{1,0:T(8,128)(2,1)} %param.13), kind=kOutput, calls=%fused_computation.37 | convolution fusion | flops 2147483648 | bytes 13107200 | tf_op jit(solution)/shard_map/hic,cd->hid/dot_general | solution.py:144
  371.3 82.8 %reduce-scatter.2.cloned.1.call-done = f32[2,256,1024]{2,1,0:T(8,128)} async-done(((f32[2,256,4096]{2,1,0:T(8,128)}), f32[2,256,1024]{2,1,0:T(8,128)}) %reduce-scatter.2.cloned.1.call-update) | async-done | bytes 2097168 | tf_op jit(solution)/shard_map/reduce_scatter | solution.py:147
  454.1 2.7 convert_bitcast_fusion
  (85 shorter events, 2.1 us)
Async XLA Ops:
  19.9 13.4 %copy-start = (bf16[1,2,256,128]{3,2,1,0:T(8,128)(2,1)S(1)}, bf16[1,2,256,128]{3,2,1,0:T(8,128)(2,1)}, u32[]{:S(2)}) copy-start(bf16[1,2,256,128]{3,2,1,0:T(8,128)(2,1)} %param.10) | copy-start | bytes 393220
  19.9 13.4 %copy-start.1 = (bf16[1,2,256,128]{3,2,1,0:T(8,128)(2,1)S(1)}, bf16[1,2,256,128]{3,2,1,0:T(8,128)(2,1)}, u32[]{:S(2)}) copy-start(bf16[1,2,256,128]{3,2,1,0:T(8,128)(2,1)} %param.9) | copy-start | bytes 393220
  19.9 15.9 %copy-start.2 = (s32[4,64]{1,0:T(4,128)S(1)}, s32[4,64]{1,0:T(4,128)}, u32[]{:S(2)}) copy-start(s32[4,64]{1,0:T(4,128)} %param.12) | copy-start | bytes 3076
  19.9 16.3 %copy-start.4 = (s32[1,64]{1,0:T(1,128)S(1)}, s32[1,64]{1,0:T(1,128)}, u32[]{:S(2)}) copy-start(s32[1,64]{1,0:T(1,128)} %param.11) | copy-start | bytes 772
  19.9 209.1 %all-to-all-start = ((bf16[64,1,2,2,128,128]{5,4,3,2,1,0:T(8,128)(2,1)}), bf16[64,1,2,2,128,128]{5,4,3,2,1,0:T(8,128)(2,1)}, u32[]{:S(2)}, u32[]{:S(2)}) async-start(bf16[64,1,2,2,128,128]{5,4,3,2,1,0:T(8,128)(2,1)} %stack.46), calls=%async_computation | async-start | bytes 16777216 | tf_op jit(solution)/shard_map/all_to_all | solution.py:71
  33.2 420.9 %reduce-scatter.2.cloned.1.call-start = ((), (), s32[]{:S(2)}) async-start(), calls=%async_computation.2 | async-start | bytes 10485760 | tf_op jit(solution)/shard_map/reduce_scatter | solution.py:147
  33.3 183.8 %collective-permute-start.1 = (bf16[2,256,128]{2,1,0:T(8,128)(2,1)S(1)}, bf16[2,256,128]{2,1,0:T(8,128)(2,1)S(1)}, u32[]{:S(2)}, u32[]{:S(2)}) collective-permute-start(bf16[2,256,128]{2,1,0:T(8,128)(2,1)S(1)} %fusion.30), channel_id=1, source_target_pairs={{4,0},{8,4},{12,8},{16,12},{20,16},{24,20},{28,24},{32,28},{36,32}... | collective-permute-start | bytes 393224 | tf_op jit(solution)/shard_map/ppermute | solution.py:14
  217.1 10.9 %collective-permute-start = (bf16[2,256,128]{2,1,0:T(8,128)(2,1)S(1)}, bf16[2,256,128]{2,1,0:T(8,128)(2,1)}, u32[]{:S(2)}, u32[]{:S(2)}) collective-permute-start(bf16[2,256,128]{2,1,0:T(8,128)(2,1)S(1)} %get-tuple-element.185), channel_id=1, source_target_pairs={{0,4},{4,8},{8,12},{12,16},{16,20},{20,24},{24,28},{28,32},{32,36}... | collective-permute-start | bytes 393224 | tf_op jit(solution)/shard_map/ppermute | solution.py:14
  239.3 6.4 %copy-start.3 = (pred[64]{0:T(512)(128)(4,1)S(1)}, pred[64]{0:T(512)(128)(4,1)}, u32[]{:S(2)}) copy-start(pred[64]{0:T(512)(128)(4,1)} %compare_and_fusion.3) | copy-start | bytes 196
Sparse Core Ops, SparseCore 0:
  371.4 82.6 reduce-scatter.1
